TPU v7x, 32 devices: a whole 2x2x4 slice. The times are simulated.
32 devices in a mesh: groups: 2 (over y), lon: 4 (over z), lat: 2 (over x), ch: 2 (over core).
Axes of the slice: x: 2, y: 2, z: 4, core: 2. Of those that a mesh axis runs over, the one named last changes fastest.
Arguments:
- features: float32 [12288, 256], P(('groups', 'lon', 'lat'), 'ch'), parts along dimension 0, may hold values from -6 to 6
- blocks: float32 [48, 3, 128, 128], P(('lon', 'lat')), may hold values from -0.3125 to 0.3125
- sources: int32 [48, 3], P(('lon', 'lat')), may hold values from 0 to 9, as said below
- live: int32 [8], P(('lon', 'lat')), may hold values from 4 to 6, as said below
- weights: float32 [4, 256, 256], P(None, None, 'ch'), may hold values from -0.1875 to 0.1875
- cotangent: float32 [12288, 256], P(('groups', 'lon', 'lat'), 'ch'), parts along dimension 0, may hold values from -6 to 6
Outputs:
- output: float32 [12288, 256], P(('groups', 'lon', 'lat'), 'ch'), parts along dimension 0
- input_grad: float32 [12288, 256], P(('groups', 'lon', 'lat'), 'ch'), parts along dimension 0
- weight_grad: float32 [8, 256, 256], P('groups', None, 'ch'), parts along dimension 0
There are 2 independent parts, one for each index of `groups`. A program takes and returns all parts, laid end to end along the dimension named above; an argument that names none is the same for every part. Nothing has to cross between parts.
Inputs may be any that keep to these rules, and one draw needn't show every extreme that they name: `sources`: on tile t of every sector and band, block 0 reads tile t itself; for t < 4, block 1 reads extended entry 6 + t; other blocks read any entry of the extended list. Bands other than the first and last are fully live; in those two, sector 0 holds 6 live tiles, sector 1 holds 4, and the others 6 - 2 to 6.
All inputs are finite; a program needn't handle non-finite values.
Results may differ from a plain program's by a relative error of at most 0.0003.
Values sent between devices are 32-bit elements; how exact they have to be, the bound alone decides.
A program may use at most 64 MiB of HBM per device.

v0:
```python
import jax
import jax.numpy as jnp
from jax import lax
from jax.sharding import PartitionSpec as P

CHEB = 4
TILE = 128
TILES = 6
highest_accuracy = lax.Precision.HIGHEST


def padded(array, sides, width, wrap):
    for axis, dim in sides:
        devices, length = (lax.axis_size(axis), array.shape[dim])
        up = [(i, (i + 1) % devices) for i in range(devices if wrap else devices - 1)]
        down = [(j, i) for i, j in up]
        last = lax.slice_in_dim(array, length - width, length, axis=dim)
        leading = lax.slice_in_dim(array, 0, width, axis=dim)
        before = lax.ppermute(last, axis, up)
        after = lax.ppermute(leading, axis, down)
        array = jnp.concatenate([before, array, after], axis=dim)
    return array


def lon_edges(paired):
    return padded(paired, (("lon", 0),), 1, True)


def lat_edges(paired):
    return padded(paired, (("lat", 0),), 1, False)


def forward_apply(pixel_field, blocks, sources, keep_mask):
    lon_padded = lon_edges(pixel_field[0:2])
    lat_padded = lat_edges(pixel_field[2:4])
    extended = jnp.concatenate(
        [pixel_field, lon_padded[0:1], lon_padded[3:4], lat_padded[0:1], lat_padded[3:4]], axis=0
    )
    selected_entries = jnp.take(extended, sources, axis=0)
    return (
        jnp.einsum("dfox,dfxk->dok", blocks, selected_entries, precision=highest_accuracy)
        * keep_mask
    )


def adjoint_apply(pixel_field, blocks, sources, keep_mask):
    share_amount = jnp.einsum(
        "yerj,yri->yeji", blocks, pixel_field * keep_mask, precision=highest_accuracy
    )
    positions = jnp.arange(TILES + 4)
    selector = (sources[:, :, None] == positions[None, None, :]).astype(jnp.float32)
    spread = jnp.einsum("tse,tsbc->ebc", selector, share_amount, precision=highest_accuracy)
    lon_padded = lon_edges(spread[TILES : TILES + 2])
    lat_padded = lat_edges(spread[TILES + 2 : TILES + 4])
    edges = jnp.concatenate(
        [lon_padded[0:1], lon_padded[3:4], lat_padded[0:1], lat_padded[3:4]], axis=0
    )
    local = spread[:TILES]
    return jnp.concatenate([local[:4] + edges, local[4:]], axis=0) * keep_mask


def recurrence(start, blocks, sources, keep_mask):
    terms = [start, forward_apply(start, blocks, sources, keep_mask)]
    for order in range(2, CHEB):
        terms.append(2.0 * forward_apply(terms[-1], blocks, sources, keep_mask) - terms[-2])
    return terms


def mix_split(term, weight_row, goal, scale):
    piece = lax.all_gather(term, "ch", axis=2, tiled=True)
    total = jnp.einsum("tpc,co->tpo", piece, weight_row, precision=highest_accuracy)
    part_grad = jnp.einsum("tpc,tpo->co", piece, goal, precision=highest_accuracy) * scale
    return (total, part_grad)


def shards(features, blocks, sources, live, weights, cotangent):
    local_in = features.shape[1]
    local_out = weights.shape[2]
    keep_mask = (jnp.arange(TILES) < live[0]).astype(jnp.float32)[:, None, None]
    pixel_field = features.reshape(TILES, TILE, local_in) * keep_mask
    goal = cotangent.reshape(TILES, TILE, local_out) * keep_mask
    scale = float(TILES * TILE * lax.axis_size("lon") * lax.axis_size("lat")) ** (-0.5)
    terms = recurrence(pixel_field, blocks, sources, keep_mask)
    output = jnp.zeros((TILES, TILE, local_out), jnp.float32)
    grads = []
    for order in range(CHEB):
        mixed, grad = mix_split(terms[order], weights[order], goal, scale)
        output = output + mixed
        grads.append(grad)
    weight_grad = jnp.stack(grads)
    weight_grad = lax.psum(weight_grad, ("lon", "lat"))
    partial_adjoint = jnp.einsum("tpo,kco->ktpc", goal, weights, precision=highest_accuracy)
    summed = lax.psum_scatter(partial_adjoint, "ch", scatter_dimension=3, tiled=True)
    adjoint = [summed[order] for order in range(CHEB)]
    for order in range(CHEB - 1, 1, -1):
        adjoint[order - 1] = adjoint[order - 1] + 2.0 * adjoint_apply(
            adjoint[order], blocks, sources, keep_mask
        )
        adjoint[order - 2] = adjoint[order - 2] - adjoint[order]
    adjoint[0] = adjoint[0] + adjoint_apply(adjoint[1], blocks, sources, keep_mask)
    input_grad = (adjoint[0] * keep_mask).reshape(TILES * TILE, local_in)
    return (output.reshape(TILES * TILE, local_out), input_grad, weight_grad)


def solution(mesh):
    placed = (
        P(("groups", "lon", "lat"), "ch"),
        P(("lon", "lat"), None, None, None),
        P(("lon", "lat"), None),
        P(("lon", "lat")),
        P(None, None, "ch"),
        P(("groups", "lon", "lat"), "ch"),
    )
    return jax.shard_map(
        shards,
        mesh=mesh,
        in_specs=placed,
        out_specs=(
            P(("groups", "lon", "lat"), "ch"),
            P(("groups", "lon", "lat"), "ch"),
            P("groups", None, "ch"),
        ),
        check_vma=False,
    )
```

profile of v0, /device:TPU:0, one launch (start us, length us, event | category | flops | bytes accessed | tf_op | source)
XLA Modules:
  0.0 199.8 jit_solution(17478462229392317581)
XLA Ops:
  8.8 1.2 copy.57
  10.0 5.4 %convolution_bitcast_fusion = f32[4,6,128,256]{2,3,1,0:T(8,128)} fusion(f32[4,256,128]{2,1,0:T(8,128)} %param.12, f32[6,128,128]{1,2,0:T(8,128)S(1)} %copy.57, f32[6]{0:T(128)S(1)} %compare_convert_fusion), kind=kOutput, calls=%fused_computation.3 | convolution fusion | flops 1208057856 | bytes 4063256 | tf_op jit(solution)/shard_map/tpo,kco->ktpc/dot_general | solution.py:92
  16.5 1.3 collective-permute-start.3
  17.8 4.8 %collective-permute-start.2 = (f32[1,128,128]{2,1,0:T(8,128)S(1)}, f32[1,128,128]{2,1,0:T(8,128)S(1)}, u32[]{:S(2)}, u32[]{:S(2)}) collective-permute-start(f32[1,128,128]{2,1,0:T(8,128)S(1)} %get-tuple-element.29), channel_id=1, source_target_pairs={{0,2},{1,3},{4,6},{5,7},{8,10},{9,11},{12,14},{13,15},{16,18},{17,... | collective-permute-start | bytes 196616 | tf_op jit(solution)/shard_map/ppermute | solution.py:19
  22.7 4.8 %collective-permute-start.1 = (f32[1,128,128]{2,1,0:T(8,128)S(1)}, f32[1,128,128]{2,1,0:T(8,128)S(1)}, u32[]{:S(2)}, u32[]{:S(2)}) collective-permute-start(f32[1,128,128]{2,1,0:T(8,128)S(1)} %get-tuple-element.30), channel_id=1, source_target_pairs={{4,0},{8,4},{12,8},{0,12},{5,1},{9,5},{13,9},{1,13},{6,2},{10,6},{... | collective-permute-start | bytes 196616 | tf_op jit(solution)/shard_map/ppermute | solution.py:20
  28.3 2.4 %all_gather.12 = f32[6,128,256]{2,1,0:T(8,128)S(1)} all-gather(f32[6,128,128]{2,1,0:T(8,128)S(1)} %get-tuple-element.5), channel_id=1, replica_groups=mesh['groups'=2,'lon'=4,'lat'=2,'ch'=2] {'ch'}, dimensions={2}, use_global_device_ids=true | all-gather | bytes 1179648 | tf_op jit(solution)/shard_map/all_gather | solution.py:70
  30.7 2.1 %fusion.35 = f32[1,256,128]{2,1,0:T(8,128)} fusion(f32[6,128,256]{2,1,0:T(8,128)S(1)} %all_gather.12, f32[6,128,128]{1,2,0:T(8,128)S(1)} %copy.57, f32[6]{0:T(128)S(1)} %compare_convert_fusion), kind=kOutput, calls=%fused_computation.43 | convolution fusion | flops 302120960 | bytes 1310744 | tf_op jit(solution)/shard_map/tpc,tpo->co/dot_general | solution.py:72
  32.9 2.4 %fusion.86 = f32[6,128,128]{2,1,0:T(8,128)} fusion(f32[6,128,256]{2,1,0:T(8,128)S(1)} %all_gather.12, f32[4,256,128]{2,1,0:T(8,128)} %param.12), kind=kOutput, calls=%fused_computation.104 | convolution fusion | flops 301989888 | bytes 1310720 | tf_op jit(solution)/shard_map/tpc,co->tpo/dot_general | solution.py:71
  35.4 1.7 gather_fusion
  37.1 1.6 copy.47
  38.7 3.2 %constant_dynamic-update-slice_fusion.9 = (f32[10,128,128]{2,1,0:T(8,128)}, f32[6,128,128]{2,1,0:T(8,128)S(1)}) fusion(f32[6]{0:T(128)S(1)} %compare_convert_fusion, f32[6,3,128,128]{3,2,1,0:T(8,128)S(1)} %copy-done, f32[6,3,128,128]{2,3,1,0:T(8,128)S(1)} %copy.47, pred[6,3]{1,0:T(8,128)(4,1)} %copy.45), kind=kOutput, calls=%fused_computation.119 | convolution fusion | flops 453378048 | bytes 3145770 | tf_op jit(solution)/shard_map/dfox,dfxk->dok/dot_general | solution.py:41
  42.0 2.5 %all_gather.13 = f32[6,128,256]{2,1,0:T(8,128)S(1)} all-gather(f32[6,128,128]{2,1,0:T(8,128)S(1)} %get-tuple-element.33), channel_id=1, replica_groups=mesh['groups'=2,'lon'=4,'lat'=2,'ch'=2] {'ch'}, dimensions={2}, use_global_device_ids=true | all-gather | bytes 1179648 | tf_op jit(solution)/shard_map/all_gather | solution.py:70
  44.5 2.4 %convolution_add_fusion.2 = f32[6,128,128]{2,1,0:T(8,128)} fusion(f32[6,128,128]{2,1,0:T(8,128)S(1)} %copy-done.5, f32[6,128,256]{2,1,0:T(8,128)S(1)} %all_gather.13, f32[4,256,128]{2,1,0:T(8,128)} %param.12), kind=kOutput, calls=%fused_computation.18 | convolution fusion | flops 302088192 | bytes 1703936 | tf_op jit(solution)/shard_map/tpc,co->tpo/dot_general | solution.py:71
  46.9 2.1 %fusion.33 = f32[1,256,128]{2,1,0:T(8,128)} fusion(f32[6,128,256]{2,1,0:T(8,128)S(1)} %all_gather.13, f32[6,128,128]{1,2,0:T(8,128)S(1)} %copy.57, f32[6]{0:T(128)S(1)} %compare_convert_fusion), kind=kOutput, calls=%fused_computation.40 | convolution fusion | flops 302120960 | bytes 1310744 | tf_op jit(solution)/shard_map/tpc,tpo->co/dot_general | solution.py:72
  49.0 1.3 collective-permute-start.7
  50.3 4.5 %collective-permute-start.6 = (f32[1,128,128]{2,1,0:T(8,128)S(1)}, f32[1,128,128]{2,1,0:T(8,128)S(1)}, u32[]{:S(2)}, u32[]{:S(2)}) collective-permute-start(f32[1,128,128]{2,1,0:T(8,128)S(1)} %get-tuple-element.25), channel_id=1, source_target_pairs={{0,2},{1,3},{4,6},{5,7},{8,10},{9,11},{12,14},{13,15},{16,18},{17,... | collective-permute-start | bytes 196616 | tf_op jit(solution)/shard_map/ppermute | solution.py:19
  54.9 4.1 %collective-permute-start.5 = (f32[1,128,128]{2,1,0:T(8,128)S(1)}, f32[1,128,128]{2,1,0:T(8,128)S(1)}, u32[]{:S(2)}, u32[]{:S(2)}) collective-permute-start(f32[1,128,128]{2,1,0:T(8,128)S(1)} %get-tuple-element.26), channel_id=1, source_target_pairs={{4,0},{8,4},{12,8},{0,12},{5,1},{9,5},{13,9},{1,13},{6,2},{10,6},{... | collective-permute-start | bytes 196616 | tf_op jit(solution)/shard_map/ppermute | solution.py:20
  59.6 1.3 collective-permute-done.5
  62.8 1.7 gather_fusion.1
  64.5 1.4 copy.51
  65.9 2.9 %constant_dynamic-update-slice_fusion.14 = (f32[10,128,128]{2,1,0:T(8,128)S(1)}, f32[6,128,128]{2,1,0:T(8,128)S(1)}) fusion(f32[6,128,128]{2,1,0:T(8,128)S(1)} %get-tuple-element.5, f32[6]{0:T(128)S(1)} %compare_convert_fusion, f32[6,3,128,128]{3,2,1,0:T(8,128)S(1)} %copy-done, f32[6,3,128,128]{2,3,1,0:T(8,128)} %copy.51, pred[6,3]{1,0:T(8,128)(4,1)} %copy.45), kind=kOutput, calls=%fused_computation.124 | convolution fusion | flops 453574656 | bytes 3538986 | tf_op jit(solution)/shard_map/dfox,dfxk->dok/dot_general | solution.py:41
  68.9 1.4 collective-permute-start.8
  70.3 2.4 %all_gather.14 = f32[6,128,256]{2,1,0:T(8,128)S(1)} all-gather(f32[6,128,128]{2,1,0:T(8,128)S(1)} %get-tuple-element.35), channel_id=1, replica_groups=mesh['groups'=2,'lon'=4,'lat'=2,'ch'=2] {'ch'}, dimensions={2}, use_global_device_ids=true | all-gather | bytes 1179648 | tf_op jit(solution)/shard_map/all_gather | solution.py:70
  72.6 2.4 %convolution_add_fusion.1 = f32[6,128,128]{2,1,0:T(8,128)} fusion(f32[6,128,128]{2,1,0:T(8,128)S(1)} %copy-done.6, f32[6,128,256]{2,1,0:T(8,128)S(1)} %all_gather.14, f32[4,256,128]{2,1,0:T(8,128)} %param.12), kind=kOutput, calls=%fused_computation.17 | convolution fusion | flops 302088192 | bytes 1703936 | tf_op jit(solution)/shard_map/tpc,co->tpo/dot_general | solution.py:71
  75.0 2.1 %fusion.31 = f32[1,256,128]{2,1,0:T(8,128)} fusion(f32[6,128,256]{2,1,0:T(8,128)S(1)} %all_gather.14, f32[6,128,128]{1,2,0:T(8,128)S(1)} %copy.57, f32[6]{0:T(128)S(1)} %compare_convert_fusion), kind=kOutput, calls=%fused_computation.37 | convolution fusion | flops 302120960 | bytes 1310744 | tf_op jit(solution)/shard_map/tpc,tpo->co/dot_general | solution.py:72
  77.1 1.3 collective-permute-start.11
  78.4 4.5 %collective-permute-start.10 = (f32[1,128,128]{2,1,0:T(8,128)S(1)}, f32[1,128,128]{2,1,0:T(8,128)S(1)}, u32[]{:S(2)}, u32[]{:S(2)}) collective-permute-start(f32[1,128,128]{2,1,0:T(8,128)S(1)} %get-tuple-element.21), channel_id=1, source_target_pairs={{0,2},{1,3},{4,6},{5,7},{8,10},{9,11},{12,14},{13,15},{16,18},{17,... | collective-permute-start | bytes 196616 | tf_op jit(solution)/shard_map/ppermute | solution.py:19
  83.0 3.1 %collective-permute-start.9 = (f32[1,128,128]{2,1,0:T(8,128)S(1)}, f32[1,128,128]{2,1,0:T(8,128)S(1)}, u32[]{:S(2)}, u32[]{:S(2)}) collective-permute-start(f32[1,128,128]{2,1,0:T(8,128)S(1)} %get-tuple-element.22), channel_id=1, source_target_pairs={{4,0},{8,4},{12,8},{0,12},{5,1},{9,5},{13,9},{1,13},{6,2},{10,6},{... | collective-permute-start | bytes 196616 | tf_op jit(solution)/shard_map/ppermute | solution.py:20
  86.1 1.9 collective-permute-done.9
  88.0 1.7 gather_fusion.2
  89.7 1.6 copy.55
  91.3 1.7 fusion.24
  93.1 2.7 %all_gather.15 = f32[6,128,256]{2,1,0:T(8,128)S(1)} all-gather(f32[6,128,128]{2,1,0:T(8,128)S(1)} %fusion.24), channel_id=1, replica_groups=mesh['groups'=2,'lon'=4,'lat'=2,'ch'=2] {'ch'}, dimensions={2}, use_global_device_ids=true | all-gather | bytes 1179648 | tf_op jit(solution)/shard_map/all_gather | solution.py:70
  95.8 1.4 fusion.29
  97.2 2.4 %convolution_add_fusion = f32[6,128,128]{2,1,0:T(8,128)} fusion(f32[6,128,128]{2,1,0:T(8,128)S(1)} %copy-done.7, f32[6,128,256]{2,1,0:T(8,128)S(1)} %all_gather.15, f32[4,256,128]{2,1,0:T(8,128)} %param.12), kind=kOutput, calls=%fused_computation.16 | convolution fusion | flops 302088192 | bytes 1703936 | tf_op jit(solution)/shard_map/tpc,co->tpo/dot_general | solution.py:71
  99.7 3.2 %fusion.55 = f32[6,128,3,128]{3,1,2,0:T(8,128)} fusion(f32[6,3,128,128]{3,2,1,0:T(8,128)S(1)} %copy-done, f32[4,6,128,128]{2,3,1,0:T(8,128)} %reduce-scatter.2.cloned.1.call-done, f32[6]{0:T(128)S(1)} %compare_convert_fusion), kind=kOutput, calls=%fused_computation.67 | convolution fusion | flops 453083136 | bytes 2752536 | tf_op jit(solution)/shard_map/yerj,yri->yeji/dot_general | solution.py:47
  102.9 1.8 copy.91
  104.7 1.1 fusion.6
  107.4 4.2 %collective-permute-start.13 = (f32[1,128,128]{1,2,0:T(8,128)S(1)}, f32[1,128,128]{1,2,0:T(8,128)S(1)}, u32[]{:S(2)}, u32[]{:S(2)}) collective-permute-start(f32[1,128,128]{1,2,0:T(8,128)S(1)} %copy.113), channel_id=1, source_target_pairs={{4,0},{8,4},{12,8},{0,12},{5,1},{9,5},{13,9},{1,13},{6,2},{10,6},{... | collective-permute-start | bytes 196616 | tf_op jit(solution)/shard_map/ppermute | solution.py:20
  111.6 1.3 collective-permute-start.14
  112.9 1.3 collective-permute-start.15
  115.2 1.1 slice.223
  116.3 1.1 slice.218
  117.6 1.5 collective-permute-done.15
  119.1 1.3 collective-permute-done.12
  120.4 3.2 %fusion.53 = f32[6,128,3,128]{3,1,2,0:T(8,128)} fusion(f32[6,3,128,128]{3,2,1,0:T(8,128)S(1)} %copy-done, f32[6]{0:T(128)S(1)} %compare_convert_fusion, f32[4,6,128,128]{2,3,1,0:T(8,128)} %reduce-scatter.2.cloned.1.call-done, f32[2,128,128]{1,2,0:T(8,128)S(1)} %copy.116, f32[4,128,128]{1,2,0:T(8,128)S(1)} %maximum_add_fusion), kind=kOutput, calls=%fused_computation.65 | convolution fusion | flops 453476352 | bytes 3145752 | tf_op jit(solution)/shard_map/yerj,yri->yeji/dot_general | solution.py:47
  123.6 1.8 copy.94
  125.4 1.1 fusion.9
  128.1 1.2 collective-permute-start.17
  129.3 4.6 %collective-permute-start.18 = (f32[1,128,128]{1,2,0:T(8,128)S(1)}, f32[1,128,128]{1,2,0:T(8,128)S(1)}, u32[]{:S(2)}, u32[]{:S(2)}) collective-permute-start(f32[1,128,128]{1,2,0:T(8,128)S(1)} %copy.120), channel_id=1, source_target_pairs={{0,2},{1,3},{4,6},{5,7},{8,10},{9,11},{12,14},{13,15},{16,18},{17,... | collective-permute-start | bytes 196616 | tf_op jit(solution)/shard_map/ppermute | solution.py:19
  133.9 1.3 collective-permute-start.19
  135.2 1.2 collective-permute-start.16
  136.3 1.2 fusion.106
  138.6 1.1 slice.230
  141.6 3.4 %fusion.47 = f32[6,128,3,128]{3,1,2,0:T(8,128)} fusion(f32[6,3,128,128]{3,2,1,0:T(8,128)S(1)} %copy-done, f32[4,6,128,128]{2,3,1,0:T(8,128)} %reduce-scatter.2.cloned.1.call-done, f32[2,128,128]{1,2,0:T(8,128)S(1)} %copy.122, f32[4,128,128]{1,2,0:T(8,128)S(1)} %maximum_add_fusion.1, f32[6]{0:T(128)S(1)} %compare_convert_fusion), kind=kOutput, calls=%fused_computation.58 | convolution fusion | flops 453574656 | bytes 3538968 | tf_op jit(solution)/shard_map/yerj,yri->yeji/dot_general | solution.py:47
  144.9 1.8 copy.97
  146.7 1.1 fusion.12
  149.1 1.3 collective-permute-start.23
  150.4 4.6 %collective-permute-start.22 = (f32[1,128,128]{2,0,1:T(1,128)S(1)}, f32[1,128,128]{2,0,1:T(1,128)S(1)}, u32[]{:S(2)}, u32[]{:S(2)}) collective-permute-start(f32[1,128,128]{2,0,1:T(1,128)S(1)} %get-tuple-element.10), channel_id=1, source_target_pairs={{0,2},{1,3},{4,6},{5,7},{8,10},{9,11},{12,14},{13,15},{16,18},{17,... | collective-permute-start | bytes 196616 | tf_op jit(solution)/shard_map/ppermute | solution.py:19
  155.0 3.9 %collective-permute-start.21 = (f32[1,128,128]{2,0,1:T(1,128)S(1)}, f32[1,128,128]{2,0,1:T(1,128)S(1)}, u32[]{:S(2)}, u32[]{:S(2)}) collective-permute-start(f32[1,128,128]{2,0,1:T(1,128)S(1)} %get-tuple-element.11), channel_id=1, source_target_pairs={{4,0},{8,4},{12,8},{0,12},{5,1},{9,5},{13,9},{1,13},{6,2},{10,6},{... | collective-permute-start | bytes 196616 | tf_op jit(solution)/shard_map/ppermute | solution.py:20
  159.0 1.1 slice.236
  160.8 1.3 slice_add_fusion
  163.2 27.3 %all-reduce.2.cloned.1.call-done = f32[4,256,128]{2,1,0:T(8,128)} async-done(((f32[4,256,128]{2,1,0:T(8,128)}), f32[4,256,128]{2,1,0:T(8,128)}) %all-reduce.2.cloned.1.call-update) | async-done | bytes 524304 | tf_op jit(solution)/shard_map/psum | solution.py:91
  190.5 1.9 copy.137
  (107 shorter events, 15.2 us)
Async XLA Ops:
  8.0 30.7 %copy-start = (f32[6,3,128,128]{3,2,1,0:T(8,128)S(1)}, f32[6,3,128,128]{3,2,1,0:T(8,128)}, u32[]{:S(2)}) copy-start(f32[6,3,128,128]{3,2,1,0:T(8,128)} %param.9) | copy-start | bytes 3538948
  8.0 91.7 %reduce-scatter.2.cloned.1.call-start = ((), (), s32[]{:S(2)}) async-start(), calls=%async_computation.1 | async-start | bytes 4718592 | tf_op jit(solution)/shard_map/reduce_scatter | solution.py:93
  15.4 1.0 copy-start.11
  15.4 12.1 %copy-start.12 = (s32[6,3]{0,1:T(4,128)S(1)}, s32[6,3]{0,1:T(4,128)}, u32[]{:S(2)}) copy-start(s32[6,3]{0,1:T(4,128)} %param.10) | copy-start | bytes 220
  15.4 175.1 %all-reduce.2.cloned.1.call-start = ((), (), s32[]{:S(2)}) async-start(), calls=%async_computation.2 | async-start | bytes 1048576 | tf_op jit(solution)/shard_map/psum | solution.py:91
  16.5 18.9 %collective-permute-start.3 = (f32[1,128,128]{2,1,0:T(8,128)S(1)}, f32[1,128,128]{2,1,0:T(8,128)S(1)}, u32[]{:S(2)}, u32[]{:S(2)}) collective-permute-start(f32[1,128,128]{2,1,0:T(8,128)S(1)} %get-tuple-element.28), channel_id=1, source_target_pairs={{2,0},{3,1},{6,4},{7,5},{10,8},{11,9},{14,12},{15,13},{18,16},{19,... | collective-permute-start | bytes 196616 | tf_op jit(solution)/shard_map/ppermute | solution.py:20
  17.8 17.5 %collective-permute-start.2 = (f32[1,128,128]{2,1,0:T(8,128)S(1)}, f32[1,128,128]{2,1,0:T(8,128)S(1)}, u32[]{:S(2)}, u32[]{:S(2)}) collective-permute-start(f32[1,128,128]{2,1,0:T(8,128)S(1)} %get-tuple-element.29), channel_id=1, source_target_pairs={{0,2},{1,3},{4,6},{5,7},{8,10},{9,11},{12,14},{13,15},{16,18},{17,... | collective-permute-start | bytes 196616 | tf_op jit(solution)/shard_map/ppermute | solution.py:19
  22.7 12.7 %collective-permute-start.1 = (f32[1,128,128]{2,1,0:T(8,128)S(1)}, f32[1,128,128]{2,1,0:T(8,128)S(1)}, u32[]{:S(2)}, u32[]{:S(2)}) collective-permute-start(f32[1,128,128]{2,1,0:T(8,128)S(1)} %get-tuple-element.30), channel_id=1, source_target_pairs={{4,0},{8,4},{12,8},{0,12},{5,1},{9,5},{13,9},{1,13},{6,2},{10,6},{... | collective-permute-start | bytes 196616 | tf_op jit(solution)/shard_map/ppermute | solution.py:20
  27.5 7.8 %collective-permute-start = (f32[1,128,128]{2,1,0:T(8,128)S(1)}, f32[1,128,128]{2,1,0:T(8,128)S(1)}, u32[]{:S(2)}, u32[]{:S(2)}) collective-permute-start(f32[1,128,128]{2,1,0:T(8,128)S(1)} %get-tuple-element.31), channel_id=1, source_target_pairs={{0,4},{4,8},{8,12},{12,0},{1,5},{5,9},{9,13},{13,1},{2,6},{6,10},{... | collective-permute-start | bytes 196616 | tf_op jit(solution)/shard_map/ppermute | solution.py:19
  41.9 2.6 %copy-start.5 = (f32[6,128,128]{2,1,0:T(8,128)S(1)}, f32[6,128,128]{2,1,0:T(8,128)}, u32[]{:S(2)}) copy-start(f32[6,128,128]{2,1,0:T(8,128)} %fusion.86) | copy-start | bytes 1179652
  41.9 17.0 %collective-permute-start.4 = (f32[1,128,128]{2,1,0:T(8,128)S(1)}, f32[1,128,128]{2,1,0:T(8,128)S(1)}, u32[]{:S(2)}, u32[]{:S(2)}) collective-permute-start(f32[1,128,128]{2,1,0:T(8,128)S(1)} %get-tuple-element.27), channel_id=1, source_target_pairs={{0,4},{4,8},{8,12},{12,0},{1,5},{5,9},{9,13},{13,1},{2,6},{6,10},{... | collective-permute-start | bytes 196616 | tf_op jit(solution)/shard_map/ppermute | solution.py:19
  49.0 13.1 %collective-permute-start.7 = (f32[1,128,128]{2,1,0:T(8,128)S(1)}, f32[1,128,128]{2,1,0:T(8,128)S(1)}, u32[]{:S(2)}, u32[]{:S(2)}) collective-permute-start(f32[1,128,128]{2,1,0:T(8,128)S(1)} %get-tuple-element.24), channel_id=1, source_target_pairs={{2,0},{3,1},{6,4},{7,5},{10,8},{11,9},{14,12},{15,13},{18,16},{19,... | collective-permute-start | bytes 196616 | tf_op jit(solution)/shard_map/ppermute | solution.py:20
  50.3 11.2 %collective-permute-start.6 = (f32[1,128,128]{2,1,0:T(8,128)S(1)}, f32[1,128,128]{2,1,0:T(8,128)S(1)}, u32[]{:S(2)}, u32[]{:S(2)}) collective-permute-start(f32[1,128,128]{2,1,0:T(8,128)S(1)} %get-tuple-element.25), channel_id=1, source_target_pairs={{0,2},{1,3},{4,6},{5,7},{8,10},{9,11},{12,14},{13,15},{16,18},{17,... | collective-permute-start | bytes 196616 | tf_op jit(solution)/shard_map/ppermute | solution.py:19
  54.9 6.0 %collective-permute-start.5 = (f32[1,128,128]{2,1,0:T(8,128)S(1)}, f32[1,128,128]{2,1,0:T(8,128)S(1)}, u32[]{:S(2)}, u32[]{:S(2)}) collective-permute-start(f32[1,128,128]{2,1,0:T(8,128)S(1)} %get-tuple-element.26), channel_id=1, source_target_pairs={{4,0},{8,4},{12,8},{0,12},{5,1},{9,5},{13,9},{1,13},{6,2},{10,6},{... | collective-permute-start | bytes 196616 | tf_op jit(solution)/shard_map/ppermute | solution.py:20
  68.8 3.8 %copy-start.6 = (f32[6,128,128]{2,1,0:T(8,128)S(1)}, f32[6,128,128]{2,1,0:T(8,128)}, u32[]{:S(2)}) copy-start(f32[6,128,128]{2,1,0:T(8,128)} %convolution_add_fusion.2) | copy-start | bytes 1179652
  68.9 17.2 %collective-permute-start.8 = (f32[1,128,128]{2,1,0:T(8,128)S(1)}, f32[1,128,128]{2,1,0:T(8,128)S(1)}, u32[]{:S(2)}, u32[]{:S(2)}) collective-permute-start(f32[1,128,128]{2,1,0:T(8,128)S(1)} %get-tuple-element.23), channel_id=1, source_target_pairs={{0,4},{4,8},{8,12},{12,0},{1,5},{5,9},{9,13},{13,1},{2,6},{6,10},{... | collective-permute-start | bytes 196616 | tf_op jit(solution)/shard_map/ppermute | solution.py:19
  77.1 10.8 %collective-permute-start.11 = (f32[1,128,128]{2,1,0:T(8,128)S(1)}, f32[1,128,128]{2,1,0:T(8,128)S(1)}, u32[]{:S(2)}, u32[]{:S(2)}) collective-permute-start(f32[1,128,128]{2,1,0:T(8,128)S(1)} %get-tuple-element.20), channel_id=1, source_target_pairs={{2,0},{3,1},{6,4},{7,5},{10,8},{11,9},{14,12},{15,13},{18,16},{19,... | collective-permute-start | bytes 196616 | tf_op jit(solution)/shard_map/ppermute | solution.py:20
  78.4 9.5 %collective-permute-start.10 = (f32[1,128,128]{2,1,0:T(8,128)S(1)}, f32[1,128,128]{2,1,0:T(8,128)S(1)}, u32[]{:S(2)}, u32[]{:S(2)}) collective-permute-start(f32[1,128,128]{2,1,0:T(8,128)S(1)} %get-tuple-element.21), channel_id=1, source_target_pairs={{0,2},{1,3},{4,6},{5,7},{8,10},{9,11},{12,14},{13,15},{16,18},{17,... | collective-permute-start | bytes 196616 | tf_op jit(solution)/shard_map/ppermute | solution.py:19
  83.0 5.0 %collective-permute-start.9 = (f32[1,128,128]{2,1,0:T(8,128)S(1)}, f32[1,128,128]{2,1,0:T(8,128)S(1)}, u32[]{:S(2)}, u32[]{:S(2)}) collective-permute-start(f32[1,128,128]{2,1,0:T(8,128)S(1)} %get-tuple-element.22), channel_id=1, source_target_pairs={{4,0},{8,4},{12,8},{0,12},{5,1},{9,5},{13,9},{1,13},{6,2},{10,6},{... | collective-permute-start | bytes 196616 | tf_op jit(solution)/shard_map/ppermute | solution.py:20
  89.7 1.7 copy-start.13
  93.0 4.2 %copy-start.7 = (f32[6,128,128]{2,1,0:T(8,128)S(1)}, f32[6,128,128]{2,1,0:T(8,128)}, u32[]{:S(2)}) copy-start(f32[6,128,128]{2,1,0:T(8,128)} %convolution_add_fusion.1) | copy-start | bytes 1179652
  104.7 9.6 %copy-start.8 = (f32[1,256,128]{2,1,0:T(8,128)S(1)}, f32[1,256,128]{2,1,0:T(8,128)}, u32[]{:S(2)}) copy-start(f32[1,256,128]{2,1,0:T(8,128)} %fusion.35) | copy-start | bytes 393220
  104.7 9.6 %copy-start.9 = (f32[1,256,128]{2,1,0:T(8,128)S(1)}, f32[1,256,128]{2,1,0:T(8,128)}, u32[]{:S(2)}) copy-start(f32[1,256,128]{2,1,0:T(8,128)} %fusion.33) | copy-start | bytes 393220
  104.7 9.6 %copy-start.10 = (f32[1,256,128]{2,1,0:T(8,128)S(1)}, f32[1,256,128]{2,1,0:T(8,128)}, u32[]{:S(2)}) copy-start(f32[1,256,128]{2,1,0:T(8,128)} %fusion.31) | copy-start | bytes 393220
  105.8 1.0 copy-start.1
  107.4 10.2 %collective-permute-start.13 = (f32[1,128,128]{1,2,0:T(8,128)S(1)}, f32[1,128,128]{1,2,0:T(8,128)S(1)}, u32[]{:S(2)}, u32[]{:S(2)}) collective-permute-start(f32[1,128,128]{1,2,0:T(8,128)S(1)} %copy.113), channel_id=1, source_target_pairs={{4,0},{8,4},{12,8},{0,12},{5,1},{9,5},{13,9},{1,13},{6,2},{10,6},{... | collective-permute-start | bytes 196616 | tf_op jit(solution)/shard_map/ppermute | solution.py:20
  111.6 6.0 %collective-permute-start.14 = (f32[1,128,128]{1,2,0:T(8,128)S(1)}, f32[1,128,128]{1,2,0:T(8,128)S(1)}, u32[]{:S(2)}, u32[]{:S(2)}) collective-permute-start(f32[1,128,128]{1,2,0:T(8,128)S(1)} %copy.114), channel_id=1, source_target_pairs={{0,2},{1,3},{4,6},{5,7},{8,10},{9,11},{12,14},{13,15},{16,18},{17,... | collective-permute-start | bytes 196616 | tf_op jit(solution)/shard_map/ppermute | solution.py:19
  112.9 6.2 %collective-permute-start.15 = (f32[1,128,128]{1,2,0:T(8,128)S(1)}, f32[1,128,128]{1,2,0:T(8,128)S(1)}, u32[]{:S(2)}, u32[]{:S(2)}) collective-permute-start(f32[1,128,128]{1,2,0:T(8,128)S(1)} %copy.115), channel_id=1, source_target_pairs={{2,0},{3,1},{6,4},{7,5},{10,8},{11,9},{14,12},{15,13},{18,16},{19,... | collective-permute-start | bytes 196616 | tf_op jit(solution)/shard_map/ppermute | solution.py:20
  114.2 6.1 %collective-permute-start.12 = (f32[1,128,128]{1,2,0:T(8,128)S(1)}, f32[1,128,128]{1,2,0:T(8,128)S(1)}, u32[]{:S(2)}, u32[]{:S(2)}) collective-permute-start(f32[1,128,128]{1,2,0:T(8,128)S(1)} %copy.112), channel_id=1, source_target_pairs={{0,4},{4,8},{8,12},{12,0},{1,5},{5,9},{9,13},{13,1},{2,6},{6,10},{... | collective-permute-start | bytes 196616 | tf_op jit(solution)/shard_map/ppermute | solution.py:19
  126.5 1.0 copy-start.3
  128.1 12.9 %collective-permute-start.17 = (f32[1,128,128]{1,2,0:T(8,128)S(1)}, f32[1,128,128]{1,2,0:T(8,128)S(1)}, u32[]{:S(2)}, u32[]{:S(2)}) collective-permute-start(f32[1,128,128]{1,2,0:T(8,128)S(1)} %copy.119), channel_id=1, source_target_pairs={{4,0},{8,4},{12,8},{0,12},{5,1},{9,5},{13,9},{1,13},{6,2},{10,6},{... | collective-permute-start | bytes 196616 | tf_op jit(solution)/shard_map/ppermute | solution.py:20
  129.3 11.8 %collective-permute-start.18 = (f32[1,128,128]{1,2,0:T(8,128)S(1)}, f32[1,128,128]{1,2,0:T(8,128)S(1)}, u32[]{:S(2)}, u32[]{:S(2)}) collective-permute-start(f32[1,128,128]{1,2,0:T(8,128)S(1)} %copy.120), channel_id=1, source_target_pairs={{0,2},{1,3},{4,6},{5,7},{8,10},{9,11},{12,14},{13,15},{16,18},{17,... | collective-permute-start | bytes 196616 | tf_op jit(solution)/shard_map/ppermute | solution.py:19
  133.9 7.2 %collective-permute-start.19 = (f32[1,128,128]{1,2,0:T(8,128)S(1)}, f32[1,128,128]{1,2,0:T(8,128)S(1)}, u32[]{:S(2)}, u32[]{:S(2)}) collective-permute-start(f32[1,128,128]{1,2,0:T(8,128)S(1)} %copy.121), channel_id=1, source_target_pairs={{2,0},{3,1},{6,4},{7,5},{10,8},{11,9},{14,12},{15,13},{18,16},{19,... | collective-permute-start | bytes 196616 | tf_op jit(solution)/shard_map/ppermute | solution.py:20
  135.2 6.4 %collective-permute-start.16 = (f32[1,128,128]{1,2,0:T(8,128)S(1)}, f32[1,128,128]{1,2,0:T(8,128)S(1)}, u32[]{:S(2)}, u32[]{:S(2)}) collective-permute-start(f32[1,128,128]{1,2,0:T(8,128)S(1)} %copy.118), channel_id=1, source_target_pairs={{0,4},{4,8},{8,12},{12,0},{1,5},{5,9},{9,13},{13,1},{2,6},{6,10},{... | collective-permute-start | bytes 196616 | tf_op jit(solution)/shard_map/ppermute | solution.py:19
  147.8 1.0 copy-start.2
  149.0 11.1 %collective-permute-start.20 = (f32[1,128,128]{2,0,1:T(1,128)S(1)}, f32[1,128,128]{2,0,1:T(1,128)S(1)}, u32[]{:S(2)}, u32[]{:S(2)}) collective-permute-start(f32[1,128,128]{2,0,1:T(1,128)S(1)} %get-tuple-element.8), channel_id=1, source_target_pairs={{0,4},{4,8},{8,12},{12,0},{1,5},{5,9},{9,13},{13,1},{2,6},{6,10},{... | collective-permute-start | bytes 196616 | tf_op jit(solution)/shard_map/ppermute | solution.py:19
  149.1 11.0 %collective-permute-start.23 = (f32[1,128,128]{2,0,1:T(1,128)S(1)}, f32[1,128,128]{2,0,1:T(1,128)S(1)}, u32[]{:S(2)}, u32[]{:S(2)}) collective-permute-start(f32[1,128,128]{2,0,1:T(1,128)S(1)} %get-tuple-element.9), channel_id=1, source_target_pairs={{2,0},{3,1},{6,4},{7,5},{10,8},{11,9},{14,12},{15,13},{18,16},{19,... | collective-permute-start | bytes 196616 | tf_op jit(solution)/shard_map/ppermute | solution.py:20
  150.4 9.8 %collective-permute-start.22 = (f32[1,128,128]{2,0,1:T(1,128)S(1)}, f32[1,128,128]{2,0,1:T(1,128)S(1)}, u32[]{:S(2)}, u32[]{:S(2)}) collective-permute-start(f32[1,128,128]{2,0,1:T(1,128)S(1)} %get-tuple-element.10), channel_id=1, source_target_pairs={{0,2},{1,3},{4,6},{5,7},{8,10},{9,11},{12,14},{13,15},{16,18},{17,... | collective-permute-start | bytes 196616 | tf_op jit(solution)/shard_map/ppermute | solution.py:19
  155.0 5.8 %collective-permute-start.21 = (f32[1,128,128]{2,0,1:T(1,128)S(1)}, f32[1,128,128]{2,0,1:T(1,128)S(1)}, u32[]{:S(2)}, u32[]{:S(2)}) collective-permute-start(f32[1,128,128]{2,0,1:T(1,128)S(1)} %get-tuple-element.11), channel_id=1, source_target_pairs={{4,0},{8,4},{12,8},{0,12},{5,1},{9,5},{13,9},{1,13},{6,2},{10,6},{... | collective-permute-start | bytes 196616 | tf_op jit(solution)/shard_map/ppermute | solution.py:20
  160.1 2.2 %copy-start.4 = (f32[1,6,128,128]{3,2,1,0:T(8,128)S(1)}, f32[1,6,128,128]{3,2,1,0:T(8,128)}, u32[]{:S(2)}) copy-start(f32[1,6,128,128]{3,2,1,0:T(8,128)} %copy.61) | copy-start | bytes 1179652
Sparse Core Ops, SparseCore 0:
  15.5 13.6 reduce-scatter.1
Sparse Core Ops, SparseCore 1:
  115.3 75.2 all-reduce.1
where the time goes:
time: 201 us; the launch traced here: 200 us
  starting transfers between devices  56 us (28%)
  matrix products  43.8 us (22%)
  local copies, waits for them, and re-layouts  35.4 us (18%)
  waiting for transfers between devices  34.4 us (17%)
  between operations  16.9 us (8%)
  blocking collectives  9.94 us (5%)
  other arithmetic  3.38 us (2%)
    ppermute x12, starting transfers between devices, padded(): after = lax.ppermute(leading, axis, down)  28.9 us
    psum x1, waiting for transfers between devices, shards(): weight_grad = lax.psum(weight_grad, ('lon', 'lat'))  27.3 us
    ppermute x12, starting transfers between devices, padded(): before = lax.ppermute(last, axis, up)  27.1 us
    all_gather x4, blocking collectives, mix_split(): piece = lax.all_gather(term, 'ch', axis=2, tiled=True)  9.94 us
    dot_general x3, matrix products, adjoint_apply(): jnp.einsum('yerj,yri->yeji', blocks, pixel_field * keep_mask, precision=h...  9.78 us
    dot_general x4, matrix products, mix_split(): jnp.einsum('tpc,co->tpo', piece, weight_row, precision=highest_accuracy)  9.75 us
    gather x6, local copies, waits for them, and re-layouts, forward_apply(): selected_entries = jnp.take(extended, sources, axis=0)  9.73 us
    unnamed x50, local copies, waits for them, and re-layouts  8.95 us
  transfers between devices with their start and end apart: 26, of which 7 were waited for; matrix products, arithmetic and copies ran while one was open for 32% of the time, Pallas kernels for 0%

commit v1 on v0

--- a/solution.py
+++ b/solution.py
@@ -88,7 +88,7 @@
         output = output + mixed
         grads.append(grad)
     weight_grad = jnp.stack(grads)
-    weight_grad = lax.psum(weight_grad, ("lon", "lat"))
+    weight_grad = lax.psum(lax.psum(weight_grad, "lat"), "lon")
     partial_adjoint = jnp.einsum("tpo,kco->ktpc", goal, weights, precision=highest_accuracy)
     summed = lax.psum_scatter(partial_adjoint, "ch", scatter_dimension=3, tiled=True)
     adjoint = [summed[order] for order in range(CHEB)]

time: 201 us -> 183 us (0.910)
  waiting for transfers between devices: 34.4 us -> 14.6 us
    psum x1 -> x2, waiting for transfers between devices: 27.3 us -> 8.15 us  [shards(): weight_grad = lax.psum(lax.psum(weight_grad, 'lat'), 'lon')]
    unnamed x50 -> x48, local copies, waits for them, and re-layouts: 8.95 us -> 12.1 us
    ppermute x12, starting transfers between devices: 27.1 us -> 24.7 us  [padded(): before = lax.ppermute(last, axis, up)]
    slice x5, local copies, waits for them, and re-layouts: 5.46 us -> 3.38 us  [adjoint_apply(): return jnp.concatenate([local[:4] + edges, local[4:]], axis=0) * keep_mask]
  transfers between devices with their start and end apart: 26 -> 27, of which waited for: 7 -> 6; matrix products, arithmetic and copies ran while one was open for 32% -> 41% of each run, Pallas kernels for 0% -> 0%
where the time goes in v1:
time: 183 us; the launch traced here: 182 us
  starting transfers between devices  55.2 us (30%)
  matrix products  44.1 us (24%)
  local copies, waits for them, and re-layouts  36.9 us (20%)
  between operations  16.9 us (9%)
  waiting for transfers between devices  14.6 us (8%)
  blocking collectives  9.71 us (5%)
  other arithmetic  4.31 us (2%)
    ppermute x12, starting transfers between devices, padded(): after = lax.ppermute(leading, axis, down)  30.4 us
    ppermute x12, starting transfers between devices, padded(): before = lax.ppermute(last, axis, up)  24.7 us
    unnamed x48, local copies, waits for them, and re-layouts  12.1 us
    dot_general x4, matrix products, mix_split(): jnp.einsum('tpc,co->tpo', piece, weight_row, precision=highest_accuracy)  9.76 us
    gather x6, local copies, waits for them, and re-layouts, forward_apply(): selected_entries = jnp.take(extended, sources, axis=0)  9.72 us
    all_gather x4, blocking collectives, mix_split(): piece = lax.all_gather(term, 'ch', axis=2, tiled=True)  9.71 us
    dot_general x3, matrix products, adjoint_apply(): jnp.einsum('yerj,yri->yeji', blocks, pixel_field * keep_mask, precision=h...  8.75 us
    psum x2, waiting for transfers between devices, shards(): weight_grad = lax.psum(lax.psum(weight_grad, 'lat'), 'lon')  8.15 us
  transfers between devices with their start and end apart: 27, of which 6 were waited for; matrix products, arithmetic and copies ran while one was open for 41% of the time, Pallas kernels for 0%

profile of v1, /device:TPU:0, one launch (start us, length us, event | category | flops | bytes accessed | tf_op | source)
XLA Modules:
  0.0 181.8 jit_solution(17831640583442149257)
XLA Ops:
  8.8 1.2 copy.57
  10.0 5.4 %convolution_bitcast_fusion = f32[4,6,128,256]{2,3,1,0:T(8,128)} fusion(f32[4,256,128]{2,1,0:T(8,128)} %param.12, f32[6,128,128]{1,2,0:T(8,128)S(1)} %copy.57, f32[6]{0:T(128)S(1)} %compare_convert_fusion), kind=kOutput, calls=%fused_computation.3 | convolution fusion | flops 1208057856 | bytes 4063256 | tf_op jit(solution)/shard_map/tpo,kco->ktpc/dot_general | solution.py:92
  16.5 1.3 collective-permute-start.3
  17.8 4.8 %collective-permute-start.2 = (f32[1,128,128]{2,1,0:T(8,128)S(1)}, f32[1,128,128]{2,1,0:T(8,128)S(1)}, u32[]{:S(2)}, u32[]{:S(2)}) collective-permute-start(f32[1,128,128]{2,1,0:T(8,128)S(1)} %get-tuple-element.29), channel_id=1, source_target_pairs={{0,2},{1,3},{4,6},{5,7},{8,10},{9,11},{12,14},{13,15},{16,18},{17,... | collective-permute-start | bytes 196616 | tf_op jit(solution)/shard_map/ppermute | solution.py:19
  22.7 4.8 %collective-permute-start.1 = (f32[1,128,128]{2,1,0:T(8,128)S(1)}, f32[1,128,128]{2,1,0:T(8,128)S(1)}, u32[]{:S(2)}, u32[]{:S(2)}) collective-permute-start(f32[1,128,128]{2,1,0:T(8,128)S(1)} %get-tuple-element.30), channel_id=1, source_target_pairs={{4,0},{8,4},{12,8},{0,12},{5,1},{9,5},{13,9},{1,13},{6,2},{10,6},{... | collective-permute-start | bytes 196616 | tf_op jit(solution)/shard_map/ppermute | solution.py:20
  28.4 2.4 %all_gather.12 = f32[6,128,256]{2,1,0:T(8,128)S(1)} all-gather(f32[6,128,128]{2,1,0:T(8,128)S(1)} %get-tuple-element.5), channel_id=1, replica_groups=mesh['groups'=2,'lon'=4,'lat'=2,'ch'=2] {'ch'}, dimensions={2}, use_global_device_ids=true | all-gather | bytes 1179648 | tf_op jit(solution)/shard_map/all_gather | solution.py:70
  30.7 2.1 %fusion.35 = f32[1,256,128]{2,1,0:T(8,128)} fusion(f32[6,128,256]{2,1,0:T(8,128)S(1)} %all_gather.12, f32[6,128,128]{1,2,0:T(8,128)S(1)} %copy.57, f32[6]{0:T(128)S(1)} %compare_convert_fusion), kind=kOutput, calls=%fused_computation.43 | convolution fusion | flops 302120960 | bytes 1310744 | tf_op jit(solution)/shard_map/tpc,tpo->co/dot_general | solution.py:72
  32.9 2.4 %fusion.86 = f32[6,128,128]{2,1,0:T(8,128)} fusion(f32[6,128,256]{2,1,0:T(8,128)S(1)} %all_gather.12, f32[4,256,128]{2,1,0:T(8,128)} %param.12), kind=kOutput, calls=%fused_computation.104 | convolution fusion | flops 301989888 | bytes 1310720 | tf_op jit(solution)/shard_map/tpc,co->tpo/dot_general | solution.py:71
  35.4 1.7 gather_fusion
  37.1 1.6 copy.47
  38.8 3.2 %constant_dynamic-update-slice_fusion.9 = (f32[10,128,128]{2,1,0:T(8,128)}, f32[6,128,128]{2,1,0:T(8,128)S(1)}) fusion(f32[6]{0:T(128)S(1)} %compare_convert_fusion, f32[6,3,128,128]{3,2,1,0:T(8,128)S(1)} %copy-done, f32[6,3,128,128]{2,3,1,0:T(8,128)S(1)} %copy.47, pred[6,3]{1,0:T(8,128)(4,1)} %copy.45), kind=kOutput, calls=%fused_computation.119 | convolution fusion | flops 453378048 | bytes 3145770 | tf_op jit(solution)/shard_map/dfox,dfxk->dok/dot_general | solution.py:41
  42.0 2.5 %all_gather.13 = f32[6,128,256]{2,1,0:T(8,128)S(1)} all-gather(f32[6,128,128]{2,1,0:T(8,128)S(1)} %get-tuple-element.33), channel_id=1, replica_groups=mesh['groups'=2,'lon'=4,'lat'=2,'ch'=2] {'ch'}, dimensions={2}, use_global_device_ids=true | all-gather | bytes 1179648 | tf_op jit(solution)/shard_map/all_gather | solution.py:70
  44.5 2.4 %convolution_add_fusion.2 = f32[6,128,128]{2,1,0:T(8,128)} fusion(f32[6,128,128]{2,1,0:T(8,128)S(1)} %copy-done.4, f32[6,128,256]{2,1,0:T(8,128)S(1)} %all_gather.13, f32[4,256,128]{2,1,0:T(8,128)} %param.12), kind=kOutput, calls=%fused_computation.18 | convolution fusion | flops 302088192 | bytes 1703936 | tf_op jit(solution)/shard_map/tpc,co->tpo/dot_general | solution.py:71
  47.0 2.1 %fusion.33 = f32[1,256,128]{2,1,0:T(8,128)} fusion(f32[6,128,256]{2,1,0:T(8,128)S(1)} %all_gather.13, f32[6,128,128]{1,2,0:T(8,128)S(1)} %copy.57, f32[6]{0:T(128)S(1)} %compare_convert_fusion), kind=kOutput, calls=%fused_computation.40 | convolution fusion | flops 302120960 | bytes 1310744 | tf_op jit(solution)/shard_map/tpc,tpo->co/dot_general | solution.py:72
  49.1 1.3 collective-permute-start.7
  50.4 4.5 %collective-permute-start.6 = (f32[1,128,128]{2,1,0:T(8,128)S(1)}, f32[1,128,128]{2,1,0:T(8,128)S(1)}, u32[]{:S(2)}, u32[]{:S(2)}) collective-permute-start(f32[1,128,128]{2,1,0:T(8,128)S(1)} %get-tuple-element.25), channel_id=1, source_target_pairs={{0,2},{1,3},{4,6},{5,7},{8,10},{9,11},{12,14},{13,15},{16,18},{17,... | collective-permute-start | bytes 196616 | tf_op jit(solution)/shard_map/ppermute | solution.py:19
  54.9 4.0 %collective-permute-start.5 = (f32[1,128,128]{2,1,0:T(8,128)S(1)}, f32[1,128,128]{2,1,0:T(8,128)S(1)}, u32[]{:S(2)}, u32[]{:S(2)}) collective-permute-start(f32[1,128,128]{2,1,0:T(8,128)S(1)} %get-tuple-element.26), channel_id=1, source_target_pairs={{4,0},{8,4},{12,8},{0,12},{5,1},{9,5},{13,9},{1,13},{6,2},{10,6},{... | collective-permute-start | bytes 196616 | tf_op jit(solution)/shard_map/ppermute | solution.py:20
  59.6 1.3 collective-permute-done.5
  62.7 1.7 gather_fusion.1
  64.5 1.4 copy.51
  65.9 3.0 %constant_dynamic-update-slice_fusion.14 = (f32[10,128,128]{2,1,0:T(8,128)S(1)}, f32[6,128,128]{2,1,0:T(8,128)S(1)}) fusion(f32[6,128,128]{2,1,0:T(8,128)S(1)} %get-tuple-element.5, f32[6]{0:T(128)S(1)} %compare_convert_fusion, f32[6,3,128,128]{3,2,1,0:T(8,128)S(1)} %copy-done, f32[6,3,128,128]{2,3,1,0:T(8,128)} %copy.51, pred[6,3]{1,0:T(8,128)(4,1)} %copy.45), kind=kOutput, calls=%fused_computation.124 | convolution fusion | flops 453574656 | bytes 3538986 | tf_op jit(solution)/shard_map/dfox,dfxk->dok/dot_general | solution.py:41
  68.9 1.4 collective-permute-start.8
  70.2 2.4 %all_gather.14 = f32[6,128,256]{2,1,0:T(8,128)S(1)} all-gather(f32[6,128,128]{2,1,0:T(8,128)S(1)} %get-tuple-element.35), channel_id=1, replica_groups=mesh['groups'=2,'lon'=4,'lat'=2,'ch'=2] {'ch'}, dimensions={2}, use_global_device_ids=true | all-gather | bytes 1179648 | tf_op jit(solution)/shard_map/all_gather | solution.py:70
  72.6 2.4 %convolution_add_fusion.1 = f32[6,128,128]{2,1,0:T(8,128)} fusion(f32[6,128,128]{2,1,0:T(8,128)S(1)} %copy-done.6, f32[6,128,256]{2,1,0:T(8,128)S(1)} %all_gather.14, f32[4,256,128]{2,1,0:T(8,128)} %param.12), kind=kOutput, calls=%fused_computation.17 | convolution fusion | flops 302088192 | bytes 1703936 | tf_op jit(solution)/shard_map/tpc,co->tpo/dot_general | solution.py:71
  75.0 2.1 %fusion.31 = f32[1,256,128]{2,1,0:T(8,128)} fusion(f32[6,128,256]{2,1,0:T(8,128)S(1)} %all_gather.14, f32[6,128,128]{1,2,0:T(8,128)S(1)} %copy.57, f32[6]{0:T(128)S(1)} %compare_convert_fusion), kind=kOutput, calls=%fused_computation.37 | convolution fusion | flops 302120960 | bytes 1310744 | tf_op jit(solution)/shard_map/tpc,tpo->co/dot_general | solution.py:72
  77.1 1.3 collective-permute-start.11
  78.4 4.5 %collective-permute-start.10 = (f32[1,128,128]{2,1,0:T(8,128)S(1)}, f32[1,128,128]{2,1,0:T(8,128)S(1)}, u32[]{:S(2)}, u32[]{:S(2)}) collective-permute-start(f32[1,128,128]{2,1,0:T(8,128)S(1)} %get-tuple-element.21), channel_id=1, source_target_pairs={{0,2},{1,3},{4,6},{5,7},{8,10},{9,11},{12,14},{13,15},{16,18},{17,... | collective-permute-start | bytes 196616 | tf_op jit(solution)/shard_map/ppermute | solution.py:19
  83.0 3.1 %collective-permute-start.9 = (f32[1,128,128]{2,1,0:T(8,128)S(1)}, f32[1,128,128]{2,1,0:T(8,128)S(1)}, u32[]{:S(2)}, u32[]{:S(2)}) collective-permute-start(f32[1,128,128]{2,1,0:T(8,128)S(1)} %get-tuple-element.22), channel_id=1, source_target_pairs={{4,0},{8,4},{12,8},{0,12},{5,1},{9,5},{13,9},{1,13},{6,2},{10,6},{... | collective-permute-start | bytes 196616 | tf_op jit(solution)/shard_map/ppermute | solution.py:20
  86.0 1.9 %collective-permute-done.9 = f32[1,128,128]{2,1,0:T(8,128)S(1)} collective-permute-done((f32[1,128,128]{2,1,0:T(8,128)S(1)}, f32[1,128,128]{2,1,0:T(8,128)S(1)}, u32[]{:S(2)}, u32[]{:S(2)}) %collective-permute-start.9) | collective-permute-done | bytes 65568 | tf_op jit(solution)/shard_map/ppermute | solution.py:20
  88.0 1.7 gather_fusion.2
  89.6 1.6 copy.55
  91.3 1.7 fusion.24
  93.0 2.5 %all_gather.15 = f32[6,128,256]{2,1,0:T(8,128)S(1)} all-gather(f32[6,128,128]{2,1,0:T(8,128)S(1)} %fusion.24), channel_id=1, replica_groups=mesh['groups'=2,'lon'=4,'lat'=2,'ch'=2] {'ch'}, dimensions={2}, use_global_device_ids=true | all-gather | bytes 1179648 | tf_op jit(solution)/shard_map/all_gather | solution.py:70
  95.5 1.4 fusion.29
  97.9 2.2 %fusion.55 = f32[6,128,3,128]{3,1,2,0:T(8,128)S(1)} fusion(f32[6,3,128,128]{3,2,1,0:T(8,128)S(1)} %copy-done, f32[4,6,128,128]{2,3,1,0:T(8,128)} %reduce-scatter.2.cloned.1.call-done, f32[6]{0:T(128)S(1)} %compare_convert_fusion), kind=kOutput, calls=%fused_computation.67 | convolution fusion | flops 453083136 | bytes 2752536 | tf_op jit(solution)/shard_map/yerj,yri->yeji/dot_general | solution.py:47
  100.1 1.7 copy.91
  101.7 2.5 %fusion.6 = f32[10,128,128]{2,0,1:T(8,128)S(1)} fusion(f32[6,128,3,128]{1,0,2,3:T(8,128)} %copy.91, s32[6,3]{0,1:T(4,128)S(1)} %copy-done.11), kind=kOutput, calls=%fused_computation.10 | convolution fusion | flops 35389620 | bytes 1835080 | tf_op jit(solution)/shard_map/tse,tsbc->ebc/dot_general | solution.py:52
  105.1 1.6 copy.112
  106.6 1.6 copy.115
  109.6 4.2 %collective-permute-start.13 = (f32[1,128,128]{1,2,0:T(8,128)}, f32[1,128,128]{1,2,0:T(8,128)}, u32[]{:S(2)}, u32[]{:S(2)}) collective-permute-start(f32[1,128,128]{1,2,0:T(8,128)} %copy.113), channel_id=1, source_target_pairs={{4,0},{8,4},{12,8},{0,12},{5,1},{9,5},{13,9},{1,13},{6,2},{10,6},{... | collective-permute-start | bytes 196616 | tf_op jit(solution)/shard_map/ppermute | solution.py:20
  113.8 1.9 %collective-permute-start.14 = (f32[1,128,128]{1,2,0:T(8,128)}, f32[1,128,128]{1,2,0:T(8,128)}, u32[]{:S(2)}, u32[]{:S(2)}) collective-permute-start(f32[1,128,128]{1,2,0:T(8,128)} %copy.114), channel_id=1, source_target_pairs={{0,2},{1,3},{4,6},{5,7},{8,10},{9,11},{12,14},{13,15},{16,18},{17,... | collective-permute-start | bytes 196616 | tf_op jit(solution)/shard_map/ppermute | solution.py:19
  115.7 1.3 collective-permute-start.15
  117.3 2.4 %convolution_add_fusion = f32[6,128,128]{2,1,0:T(8,128)} fusion(f32[6,128,128]{2,1,0:T(8,128)S(1)} %copy-done.5, f32[6,128,256]{2,1,0:T(8,128)S(1)} %all_gather.15, f32[4,256,128]{2,1,0:T(8,128)} %param.12), kind=kOutput, calls=%fused_computation.16 | convolution fusion | flops 302088192 | bytes 1703936 | tf_op jit(solution)/shard_map/tpc,co->tpo/dot_general | solution.py:71
  119.7 8.2 %all-reduce.3.cloned.1.call-done = f32[4,256,128]{2,1,0:T(8,128)} async-done(((f32[4,256,128]{2,1,0:T(8,128)}), f32[4,256,128]{2,1,0:T(8,128)}) %all-reduce.3.cloned.1.call-update) | async-done | bytes 524304 | tf_op jit(solution)/shard_map/psum | solution.py:91
  129.3 3.2 %fusion.53 = f32[6,128,3,128]{3,1,2,0:T(8,128)} fusion(f32[6,3,128,128]{3,2,1,0:T(8,128)S(1)} %copy-done, f32[6]{0:T(128)S(1)} %compare_convert_fusion, f32[4,6,128,128]{2,3,1,0:T(8,128)} %reduce-scatter.2.cloned.1.call-done, f32[2,128,128]{1,2,0:T(8,128)S(1)} %copy.116, f32[4,128,128]{1,2,0:T(8,128)S(1)} %maximum_add_fusion), kind=kOutput, calls=%fused_computation.65 | convolution fusion | flops 453476352 | bytes 3145752 | tf_op jit(solution)/shard_map/yerj,yri->yeji/dot_general | solution.py:47
  132.5 1.8 copy.94
  134.3 1.1 fusion.9
  137.0 2.7 %collective-permute-start.17 = (f32[1,128,128]{1,2,0:T(8,128)S(1)}, f32[1,128,128]{1,2,0:T(8,128)S(1)}, u32[]{:S(2)}, u32[]{:S(2)}) collective-permute-start(f32[1,128,128]{1,2,0:T(8,128)S(1)} %copy.119), channel_id=1, source_target_pairs={{4,0},{8,4},{12,8},{0,12},{5,1},{9,5},{13,9},{1,13},{6,2},{10,6},{... | collective-permute-start | bytes 196616 | tf_op jit(solution)/shard_map/ppermute | solution.py:20
  139.7 2.5 %collective-permute-start.18 = (f32[1,128,128]{1,2,0:T(8,128)S(1)}, f32[1,128,128]{1,2,0:T(8,128)S(1)}, u32[]{:S(2)}, u32[]{:S(2)}) collective-permute-start(f32[1,128,128]{1,2,0:T(8,128)S(1)} %copy.120), channel_id=1, source_target_pairs={{0,2},{1,3},{4,6},{5,7},{8,10},{9,11},{12,14},{13,15},{16,18},{17,... | collective-permute-start | bytes 196616 | tf_op jit(solution)/shard_map/ppermute | solution.py:19
  142.2 1.3 collective-permute-start.19
  143.6 1.2 fusion.106
  145.8 1.1 slice.230
  146.9 1.1 slice.225
  148.4 1.4 collective-permute-done.16
  149.8 3.4 %fusion.47 = f32[6,128,3,128]{3,1,2,0:T(8,128)} fusion(f32[6,3,128,128]{3,2,1,0:T(8,128)S(1)} %copy-done, f32[4,6,128,128]{2,3,1,0:T(8,128)} %reduce-scatter.2.cloned.1.call-done, f32[2,128,128]{1,2,0:T(8,128)S(1)} %copy.122, f32[4,128,128]{1,2,0:T(8,128)S(1)} %maximum_add_fusion.1, f32[6]{0:T(128)S(1)} %compare_convert_fusion), kind=kOutput, calls=%fused_computation.58 | convolution fusion | flops 453574656 | bytes 3538968 | tf_op jit(solution)/shard_map/yerj,yri->yeji/dot_general | solution.py:47
  153.1 1.8 copy.97
  155.0 1.1 fusion.12
  157.3 1.3 collective-permute-start.23
  158.6 4.5 %collective-permute-start.22 = (f32[1,128,128]{2,0,1:T(1,128)S(1)}, f32[1,128,128]{2,0,1:T(1,128)S(1)}, u32[]{:S(2)}, u32[]{:S(2)}) collective-permute-start(f32[1,128,128]{2,0,1:T(1,128)S(1)} %get-tuple-element.10), channel_id=1, source_target_pairs={{0,2},{1,3},{4,6},{5,7},{8,10},{9,11},{12,14},{13,15},{16,18},{17,... | collective-permute-start | bytes 196616 | tf_op jit(solution)/shard_map/ppermute | solution.py:19
  163.2 3.9 %collective-permute-start.21 = (f32[1,128,128]{2,0,1:T(1,128)S(1)}, f32[1,128,128]{2,0,1:T(1,128)S(1)}, u32[]{:S(2)}, u32[]{:S(2)}) collective-permute-start(f32[1,128,128]{2,0,1:T(1,128)S(1)} %get-tuple-element.11), channel_id=1, source_target_pairs={{4,0},{8,4},{12,8},{0,12},{5,1},{9,5},{13,9},{1,13},{6,2},{10,6},{... | collective-permute-start | bytes 196616 | tf_op jit(solution)/shard_map/ppermute | solution.py:20
  167.2 1.1 slice.236
  168.4 1.7 collective-permute-done.21
  170.1 1.3 slice_add_fusion
  172.5 1.9 %copy.138 = f32[4,256,128]{2,1,0:T(8,128)} copy(f32[4,256,128]{2,1,0:T(8,128)} %all-reduce.5.cloned.1.call-done) | data formatting | bytes 1048576
  (108 shorter events, 15.2 us)
Async XLA Ops:
  8.0 30.8 %copy-start = (f32[6,3,128,128]{3,2,1,0:T(8,128)S(1)}, f32[6,3,128,128]{3,2,1,0:T(8,128)}, u32[]{:S(2)}) copy-start(f32[6,3,128,128]{3,2,1,0:T(8,128)} %param.9) | copy-start | bytes 3538948
  8.0 89.9 %reduce-scatter.2.cloned.1.call-start = ((), (), s32[]{:S(2)}) async-start(), calls=%async_computation.1 | async-start | bytes 4718592 | tf_op jit(solution)/shard_map/reduce_scatter | solution.py:93
  15.4 1.0 copy-start.10
  15.4 12.1 %copy-start.11 = (s32[6,3]{0,1:T(4,128)S(1)}, s32[6,3]{0,1:T(4,128)}, u32[]{:S(2)}) copy-start(s32[6,3]{0,1:T(4,128)} %param.10) | copy-start | bytes 220
  15.4 112.5 %all-reduce.3.cloned.1.call-start = ((), (), s32[]{:S(2)}) async-start(), calls=%async_computation.2 | async-start | bytes 1048576 | tf_op jit(solution)/shard_map/psum | solution.py:91
  16.5 18.9 %collective-permute-start.3 = (f32[1,128,128]{2,1,0:T(8,128)S(1)}, f32[1,128,128]{2,1,0:T(8,128)S(1)}, u32[]{:S(2)}, u32[]{:S(2)}) collective-permute-start(f32[1,128,128]{2,1,0:T(8,128)S(1)} %get-tuple-element.28), channel_id=1, source_target_pairs={{2,0},{3,1},{6,4},{7,5},{10,8},{11,9},{14,12},{15,13},{18,16},{19,... | collective-permute-start | bytes 196616 | tf_op jit(solution)/shard_map/ppermute | solution.py:20
  17.8 17.6 %collective-permute-start.2 = (f32[1,128,128]{2,1,0:T(8,128)S(1)}, f32[1,128,128]{2,1,0:T(8,128)S(1)}, u32[]{:S(2)}, u32[]{:S(2)}) collective-permute-start(f32[1,128,128]{2,1,0:T(8,128)S(1)} %get-tuple-element.29), channel_id=1, source_target_pairs={{0,2},{1,3},{4,6},{5,7},{8,10},{9,11},{12,14},{13,15},{16,18},{17,... | collective-permute-start | bytes 196616 | tf_op jit(solution)/shard_map/ppermute | solution.py:19
  22.7 12.7 %collective-permute-start.1 = (f32[1,128,128]{2,1,0:T(8,128)S(1)}, f32[1,128,128]{2,1,0:T(8,128)S(1)}, u32[]{:S(2)}, u32[]{:S(2)}) collective-permute-start(f32[1,128,128]{2,1,0:T(8,128)S(1)} %get-tuple-element.30), channel_id=1, source_target_pairs={{4,0},{8,4},{12,8},{0,12},{5,1},{9,5},{13,9},{1,13},{6,2},{10,6},{... | collective-permute-start | bytes 196616 | tf_op jit(solution)/shard_map/ppermute | solution.py:20
  27.5 7.9 %collective-permute-start = (f32[1,128,128]{2,1,0:T(8,128)S(1)}, f32[1,128,128]{2,1,0:T(8,128)S(1)}, u32[]{:S(2)}, u32[]{:S(2)}) collective-permute-start(f32[1,128,128]{2,1,0:T(8,128)S(1)} %get-tuple-element.31), channel_id=1, source_target_pairs={{0,4},{4,8},{8,12},{12,0},{1,5},{5,9},{9,13},{13,1},{2,6},{6,10},{... | collective-permute-start | bytes 196616 | tf_op jit(solution)/shard_map/ppermute | solution.py:19
  41.9 2.6 %copy-start.4 = (f32[6,128,128]{2,1,0:T(8,128)S(1)}, f32[6,128,128]{2,1,0:T(8,128)}, u32[]{:S(2)}) copy-start(f32[6,128,128]{2,1,0:T(8,128)} %fusion.86) | copy-start | bytes 1179652
  41.9 17.0 %collective-permute-start.4 = (f32[1,128,128]{2,1,0:T(8,128)S(1)}, f32[1,128,128]{2,1,0:T(8,128)S(1)}, u32[]{:S(2)}, u32[]{:S(2)}) collective-permute-start(f32[1,128,128]{2,1,0:T(8,128)S(1)} %get-tuple-element.27), channel_id=1, source_target_pairs={{0,4},{4,8},{8,12},{12,0},{1,5},{5,9},{9,13},{13,1},{2,6},{6,10},{... | collective-permute-start | bytes 196616 | tf_op jit(solution)/shard_map/ppermute | solution.py:19
  49.1 13.1 %collective-permute-start.7 = (f32[1,128,128]{2,1,0:T(8,128)S(1)}, f32[1,128,128]{2,1,0:T(8,128)S(1)}, u32[]{:S(2)}, u32[]{:S(2)}) collective-permute-start(f32[1,128,128]{2,1,0:T(8,128)S(1)} %get-tuple-element.24), channel_id=1, source_target_pairs={{2,0},{3,1},{6,4},{7,5},{10,8},{11,9},{14,12},{15,13},{18,16},{19,... | collective-permute-start | bytes 196616 | tf_op jit(solution)/shard_map/ppermute | solution.py:20
  50.4 11.1 %collective-permute-start.6 = (f32[1,128,128]{2,1,0:T(8,128)S(1)}, f32[1,128,128]{2,1,0:T(8,128)S(1)}, u32[]{:S(2)}, u32[]{:S(2)}) collective-permute-start(f32[1,128,128]{2,1,0:T(8,128)S(1)} %get-tuple-element.25), channel_id=1, source_target_pairs={{0,2},{1,3},{4,6},{5,7},{8,10},{9,11},{12,14},{13,15},{16,18},{17,... | collective-permute-start | bytes 196616 | tf_op jit(solution)/shard_map/ppermute | solution.py:19
  54.9 6.0 %collective-permute-start.5 = (f32[1,128,128]{2,1,0:T(8,128)S(1)}, f32[1,128,128]{2,1,0:T(8,128)S(1)}, u32[]{:S(2)}, u32[]{:S(2)}) collective-permute-start(f32[1,128,128]{2,1,0:T(8,128)S(1)} %get-tuple-element.26), channel_id=1, source_target_pairs={{4,0},{8,4},{12,8},{0,12},{5,1},{9,5},{13,9},{1,13},{6,2},{10,6},{... | collective-permute-start | bytes 196616 | tf_op jit(solution)/shard_map/ppermute | solution.py:20
  68.8 3.8 %copy-start.6 = (f32[6,128,128]{2,1,0:T(8,128)S(1)}, f32[6,128,128]{2,1,0:T(8,128)}, u32[]{:S(2)}) copy-start(f32[6,128,128]{2,1,0:T(8,128)} %convolution_add_fusion.2) | copy-start | bytes 1179652
  68.9 17.2 %collective-permute-start.8 = (f32[1,128,128]{2,1,0:T(8,128)S(1)}, f32[1,128,128]{2,1,0:T(8,128)S(1)}, u32[]{:S(2)}, u32[]{:S(2)}) collective-permute-start(f32[1,128,128]{2,1,0:T(8,128)S(1)} %get-tuple-element.23), channel_id=1, source_target_pairs={{0,4},{4,8},{8,12},{12,0},{1,5},{5,9},{9,13},{13,1},{2,6},{6,10},{... | collective-permute-start | bytes 196616 | tf_op jit(solution)/shard_map/ppermute | solution.py:19
  77.1 10.8 %collective-permute-start.11 = (f32[1,128,128]{2,1,0:T(8,128)S(1)}, f32[1,128,128]{2,1,0:T(8,128)S(1)}, u32[]{:S(2)}, u32[]{:S(2)}) collective-permute-start(f32[1,128,128]{2,1,0:T(8,128)S(1)} %get-tuple-element.20), channel_id=1, source_target_pairs={{2,0},{3,1},{6,4},{7,5},{10,8},{11,9},{14,12},{15,13},{18,16},{19,... | collective-permute-start | bytes 196616 | tf_op jit(solution)/shard_map/ppermute | solution.py:20
  78.4 9.5 %collective-permute-start.10 = (f32[1,128,128]{2,1,0:T(8,128)S(1)}, f32[1,128,128]{2,1,0:T(8,128)S(1)}, u32[]{:S(2)}, u32[]{:S(2)}) collective-permute-start(f32[1,128,128]{2,1,0:T(8,128)S(1)} %get-tuple-element.21), channel_id=1, source_target_pairs={{0,2},{1,3},{4,6},{5,7},{8,10},{9,11},{12,14},{13,15},{16,18},{17,... | collective-permute-start | bytes 196616 | tf_op jit(solution)/shard_map/ppermute | solution.py:19
  83.0 5.0 %collective-permute-start.9 = (f32[1,128,128]{2,1,0:T(8,128)S(1)}, f32[1,128,128]{2,1,0:T(8,128)S(1)}, u32[]{:S(2)}, u32[]{:S(2)}) collective-permute-start(f32[1,128,128]{2,1,0:T(8,128)S(1)} %get-tuple-element.22), channel_id=1, source_target_pairs={{4,0},{8,4},{12,8},{0,12},{5,1},{9,5},{13,9},{1,13},{6,2},{10,6},{... | collective-permute-start | bytes 196616 | tf_op jit(solution)/shard_map/ppermute | solution.py:20
  89.6 1.6 copy-start.12
  93.0 4.0 %copy-start.7 = (f32[1,256,128]{2,1,0:T(8,128)S(1)}, f32[1,256,128]{2,1,0:T(8,128)}, u32[]{:S(2)}) copy-start(f32[1,256,128]{2,1,0:T(8,128)} %fusion.35) | copy-start | bytes 393220
  93.0 4.0 %copy-start.8 = (f32[1,256,128]{2,1,0:T(8,128)S(1)}, f32[1,256,128]{2,1,0:T(8,128)}, u32[]{:S(2)}) copy-start(f32[1,256,128]{2,1,0:T(8,128)} %fusion.33) | copy-start | bytes 393220
  93.0 4.0 %copy-start.9 = (f32[1,256,128]{2,1,0:T(8,128)S(1)}, f32[1,256,128]{2,1,0:T(8,128)}, u32[]{:S(2)}) copy-start(f32[1,256,128]{2,1,0:T(8,128)} %fusion.31) | copy-start | bytes 393220
  97.8 74.7 %all-reduce.5.cloned.1.call-start = ((), (), s32[]{:S(2)}) async-start(), calls=%async_computation.3 | async-start | bytes 1048576 | tf_op jit(solution)/shard_map/psum | solution.py:91
  104.2 13.0 %copy-start.5 = (f32[6,128,128]{2,1,0:T(8,128)S(1)}, f32[6,128,128]{2,1,0:T(8,128)}, u32[]{:S(2)}) copy-start(f32[6,128,128]{2,1,0:T(8,128)} %convolution_add_fusion.1) | copy-start | bytes 1179652
  109.6 18.7 %collective-permute-start.13 = (f32[1,128,128]{1,2,0:T(8,128)}, f32[1,128,128]{1,2,0:T(8,128)}, u32[]{:S(2)}, u32[]{:S(2)}) collective-permute-start(f32[1,128,128]{1,2,0:T(8,128)} %copy.113), channel_id=1, source_target_pairs={{4,0},{8,4},{12,8},{0,12},{5,1},{9,5},{13,9},{1,13},{6,2},{10,6},{... | collective-permute-start | bytes 196616 | tf_op jit(solution)/shard_map/ppermute | solution.py:20
  113.8 14.5 %collective-permute-start.14 = (f32[1,128,128]{1,2,0:T(8,128)}, f32[1,128,128]{1,2,0:T(8,128)}, u32[]{:S(2)}, u32[]{:S(2)}) collective-permute-start(f32[1,128,128]{1,2,0:T(8,128)} %copy.114), channel_id=1, source_target_pairs={{0,2},{1,3},{4,6},{5,7},{8,10},{9,11},{12,14},{13,15},{16,18},{17,... | collective-permute-start | bytes 196616 | tf_op jit(solution)/shard_map/ppermute | solution.py:19
  115.7 12.6 %collective-permute-start.15 = (f32[1,128,128]{1,2,0:T(8,128)}, f32[1,128,128]{1,2,0:T(8,128)}, u32[]{:S(2)}, u32[]{:S(2)}) collective-permute-start(f32[1,128,128]{1,2,0:T(8,128)} %copy.115), channel_id=1, source_target_pairs={{2,0},{3,1},{6,4},{7,5},{10,8},{11,9},{14,12},{15,13},{18,16},{19,... | collective-permute-start | bytes 196616 | tf_op jit(solution)/shard_map/ppermute | solution.py:20
  117.0 11.3 %collective-permute-start.12 = (f32[1,128,128]{1,2,0:T(8,128)}, f32[1,128,128]{1,2,0:T(8,128)}, u32[]{:S(2)}, u32[]{:S(2)}) collective-permute-start(f32[1,128,128]{1,2,0:T(8,128)} %copy.112), channel_id=1, source_target_pairs={{0,4},{4,8},{8,12},{12,0},{1,5},{5,9},{9,13},{13,1},{2,6},{6,10},{... | collective-permute-start | bytes 196616 | tf_op jit(solution)/shard_map/ppermute | solution.py:19
  135.4 1.0 copy-start.2
  137.0 11.2 %collective-permute-start.17 = (f32[1,128,128]{1,2,0:T(8,128)S(1)}, f32[1,128,128]{1,2,0:T(8,128)S(1)}, u32[]{:S(2)}, u32[]{:S(2)}) collective-permute-start(f32[1,128,128]{1,2,0:T(8,128)S(1)} %copy.119), channel_id=1, source_target_pairs={{4,0},{8,4},{12,8},{0,12},{5,1},{9,5},{13,9},{1,13},{6,2},{10,6},{... | collective-permute-start | bytes 196616 | tf_op jit(solution)/shard_map/ppermute | solution.py:20
  139.7 8.5 %collective-permute-start.18 = (f32[1,128,128]{1,2,0:T(8,128)S(1)}, f32[1,128,128]{1,2,0:T(8,128)S(1)}, u32[]{:S(2)}, u32[]{:S(2)}) collective-permute-start(f32[1,128,128]{1,2,0:T(8,128)S(1)} %copy.120), channel_id=1, source_target_pairs={{0,2},{1,3},{4,6},{5,7},{8,10},{9,11},{12,14},{13,15},{16,18},{17,... | collective-permute-start | bytes 196616 | tf_op jit(solution)/shard_map/ppermute | solution.py:19
  142.2 6.2 %collective-permute-start.19 = (f32[1,128,128]{1,2,0:T(8,128)S(1)}, f32[1,128,128]{1,2,0:T(8,128)S(1)}, u32[]{:S(2)}, u32[]{:S(2)}) collective-permute-start(f32[1,128,128]{1,2,0:T(8,128)S(1)} %copy.121), channel_id=1, source_target_pairs={{2,0},{3,1},{6,4},{7,5},{10,8},{11,9},{14,12},{15,13},{18,16},{19,... | collective-permute-start | bytes 196616 | tf_op jit(solution)/shard_map/ppermute | solution.py:20
  143.5 6.2 %collective-permute-start.16 = (f32[1,128,128]{1,2,0:T(8,128)S(1)}, f32[1,128,128]{1,2,0:T(8,128)S(1)}, u32[]{:S(2)}, u32[]{:S(2)}) collective-permute-start(f32[1,128,128]{1,2,0:T(8,128)S(1)} %copy.118), channel_id=1, source_target_pairs={{0,4},{4,8},{8,12},{12,0},{1,5},{5,9},{9,13},{13,1},{2,6},{6,10},{... | collective-permute-start | bytes 196616 | tf_op jit(solution)/shard_map/ppermute | solution.py:19
  156.1 1.0 copy-start.1
  157.3 11.1 %collective-permute-start.20 = (f32[1,128,128]{2,0,1:T(1,128)S(1)}, f32[1,128,128]{2,0,1:T(1,128)S(1)}, u32[]{:S(2)}, u32[]{:S(2)}) collective-permute-start(f32[1,128,128]{2,0,1:T(1,128)S(1)} %get-tuple-element.8), channel_id=1, source_target_pairs={{0,4},{4,8},{8,12},{12,0},{1,5},{5,9},{9,13},{13,1},{2,6},{6,10},{... | collective-permute-start | bytes 196616 | tf_op jit(solution)/shard_map/ppermute | solution.py:19
  157.3 11.0 %collective-permute-start.23 = (f32[1,128,128]{2,0,1:T(1,128)S(1)}, f32[1,128,128]{2,0,1:T(1,128)S(1)}, u32[]{:S(2)}, u32[]{:S(2)}) collective-permute-start(f32[1,128,128]{2,0,1:T(1,128)S(1)} %get-tuple-element.9), channel_id=1, source_target_pairs={{2,0},{3,1},{6,4},{7,5},{10,8},{11,9},{14,12},{15,13},{18,16},{19,... | collective-permute-start | bytes 196616 | tf_op jit(solution)/shard_map/ppermute | solution.py:20
  158.6 9.7 %collective-permute-start.22 = (f32[1,128,128]{2,0,1:T(1,128)S(1)}, f32[1,128,128]{2,0,1:T(1,128)S(1)}, u32[]{:S(2)}, u32[]{:S(2)}) collective-permute-start(f32[1,128,128]{2,0,1:T(1,128)S(1)} %get-tuple-element.10), channel_id=1, source_target_pairs={{0,2},{1,3},{4,6},{5,7},{8,10},{9,11},{12,14},{13,15},{16,18},{17,... | collective-permute-start | bytes 196616 | tf_op jit(solution)/shard_map/ppermute | solution.py:19
  163.2 6.9 %collective-permute-start.21 = (f32[1,128,128]{2,0,1:T(1,128)S(1)}, f32[1,128,128]{2,0,1:T(1,128)S(1)}, u32[]{:S(2)}, u32[]{:S(2)}) collective-permute-start(f32[1,128,128]{2,0,1:T(1,128)S(1)} %get-tuple-element.11), channel_id=1, source_target_pairs={{4,0},{8,4},{12,8},{0,12},{5,1},{9,5},{13,9},{1,13},{6,2},{10,6},{... | collective-permute-start | bytes 196616 | tf_op jit(solution)/shard_map/ppermute | solution.py:20
  168.3 3.3 %copy-start.3 = (f32[1,6,128,128]{3,2,1,0:T(8,128)S(1)}, f32[1,6,128,128]{3,2,1,0:T(8,128)}, u32[]{:S(2)}) copy-start(f32[1,6,128,128]{3,2,1,0:T(8,128)} %copy.61) | copy-start | bytes 1179652
Sparse Core Ops, SparseCore 0:
  15.5 13.6 reduce-scatter.1
Sparse Core Ops, SparseCore 1:
  97.9 29.9 all-reduce.2
  130.1 40.8 all-reduce.4
